TPU v7x, 256 devices: a whole 4x4x8 slice. The times are simulated.
256 devices in a mesh: dp: 16 (over x, y), tensor: 16 (over z, core).
Axes of the slice: x: 4, y: 4, z: 8, core: 2. Of those that a mesh axis runs over, the one named last changes fastest.
Arguments:
- activations: bfloat16 [12288, 8192], P('dp', 'tensor'), may hold values from -6 to 6
- query_gradient: bfloat16 [12288, 8192], P('dp', 'tensor'), may hold values from -6 to 6
- query_matrix: bfloat16 [8192, 8192], P(None, 'tensor'), may hold values from -0.09375 to 0.09375
- down_table_rows: bfloat16 [64, 16, 8192], P('dp', None, 'tensor'), may hold values from -3 to 3
- up_table_rows: bfloat16 [64, 16, 8192], P('dp', None, 'tensor'), may hold values from -3 to 3
- adapter_per_group: int32 [96], P('dp'), may hold values from 0 to 63
- slot_of_adapter: int32 [64], replicated, may hold values from 0 to 63, each once
Outputs:
- token_gradient: float32 [12288, 8192], P('dp', 'tensor')
- down_after_step: bfloat16 [64, 16, 8192], P(None, None, 'tensor')
- up_after_step: bfloat16 [64, 16, 8192], P(None, None, 'tensor')
Inputs may be any that keep to these rules, and one draw needn't show every extreme that they name: `slot_of_adapter`: each id appears once.
All inputs are finite; a program needn't handle non-finite values.
Results may differ from a plain program's by a relative error of at most 0.0015.
Values may be sent and summed in bfloat16 or wider, within the bound.
A program may use at most 128 MiB of HBM per device.

v0:
```python
import math

import jax
import jax.numpy as jnp
from jax import lax
from jax.sharding import PartitionSpec as P

MODEL_WIDTH = 8192
ADAPTER_RANK = 16


adapter_scale = 0.25
learning_rate = 1.5


def shards(
    activations,
    query_gradient,
    query_matrix,
    down_table_rows,
    up_table_rows,
    adapter_per_group,
    slot_of_adapter,
):
    token_rows, shard_width = activations.shape
    query_local = query_gradient.shape[1]
    group_count = adapter_per_group.shape[0]
    per_group = token_rows // group_count
    adapters = slot_of_adapter.shape[0]
    scaled_down_grad = 1.0 / math.sqrt(MODEL_WIDTH)
    scaled_up_grad = adapter_scale / math.sqrt(ADAPTER_RANK)
    table_down, table_up = (
        lax.all_gather(down_table_rows, "dp", axis=0, tiled=True),
        lax.all_gather(up_table_rows, "dp", axis=0, tiled=True),
    )
    table_position = jnp.take(slot_of_adapter, adapter_per_group, axis=0)
    selected_down = jnp.take(table_down, table_position, axis=0)
    selected_up = jnp.take(table_up, table_position, axis=0)
    grouped_x = activations.reshape(group_count, per_group, shard_width)
    grouped_dy = query_gradient.reshape(group_count, per_group, query_local)
    low_part = jnp.einsum(
        "gtd,grd->gtr", grouped_x, selected_down, preferred_element_type=jnp.float32
    )
    back_part = jnp.einsum(
        "gtq,grq->gtr", grouped_dy, selected_up, preferred_element_type=jnp.float32
    )
    low_sum, back_sum = lax.psum((low_part, back_part), "tensor")
    low = (low_sum * scaled_down_grad).astype(jnp.bfloat16)
    backward_result = (back_sum * scaled_up_grad).astype(jnp.bfloat16)
    adapter_term = jnp.einsum(
        "ivo,ios->ivs", backward_result, selected_down, preferred_element_type=jnp.float32
    )
    adapter_term = adapter_term.reshape(token_rows, shard_width) * scaled_down_grad
    partial_value = lax.dot_general(
        query_gradient, query_matrix, (((1,), (1,)), ((), ())), preferred_element_type=jnp.float32
    )
    frozen_term = lax.psum_scatter(partial_value, "tensor", scatter_dimension=1, tiled=True)
    token_gradient = frozen_term + adapter_term
    grad_a = (
        jnp.einsum("gtr,gtd->grd", backward_result, grouped_x, preferred_element_type=jnp.float32)
        * scaled_down_grad
    )
    grad_b = (
        jnp.einsum("gtr,gtq->grq", low, grouped_dy, preferred_element_type=jnp.float32)
        * scaled_up_grad
    )
    onehot = (table_position[:, None] == jnp.arange(adapters, dtype=jnp.int32)[None, :]).astype(
        jnp.float32
    )
    down_lookup = jnp.einsum("ga,grd->ard", onehot, grad_a, precision=lax.Precision.HIGHEST)
    up_lookup = jnp.einsum("ga,grq->arq", onehot, grad_b, precision=lax.Precision.HIGHEST)
    owner_down_rows, owner_up_rows = (
        lax.psum_scatter(down_lookup, "dp", scatter_dimension=0, tiled=True),
        lax.psum_scatter(up_lookup, "dp", scatter_dimension=0, tiled=True),
    )
    stepped_down = (down_table_rows.astype(jnp.float32) - learning_rate * owner_down_rows).astype(
        jnp.bfloat16
    )
    stepped_up = (up_table_rows.astype(jnp.float32) - learning_rate * owner_up_rows).astype(
        jnp.bfloat16
    )
    down_after_step, up_after_step = (
        lax.all_gather(stepped_down, "dp", axis=0, tiled=True),
        lax.all_gather(stepped_up, "dp", axis=0, tiled=True),
    )
    return (token_gradient, down_after_step, up_after_step)


def solution(mesh):
    return jax.shard_map(
        shards,
        mesh=mesh,
        in_specs=(
            P("dp", "tensor"),
            P("dp", "tensor"),
            P(None, "tensor"),
            P("dp", None, "tensor"),
            P("dp", None, "tensor"),
            P("dp"),
            P(),
        ),
        out_specs=(P("dp", "tensor"), P(None, None, "tensor"), P(None, None, "tensor")),
        check_vma=False,
    )
```

profile of v0, /device:TPU:1, one launch (start us, length us, event | category | flops | bytes accessed | tf_op | source)
XLA Modules:
  0.0 641.7 jit_solution(6845466112073198827)
XLA Ops:
  7.2 0.0 copy-start
  7.2 0.0 all-gather.5.cloned.1.call-start
  7.2 0.7 all-gather.5.cloned.1.call-update
  7.9 0.0 all-gather.7.cloned.1.call-start
  8.0 0.7 all-gather.7.cloned.1.call-update
  8.7 0.0 all-reduce.3.cloned.1.call-start
  8.7 0.7 compare_select_fusion.1
  9.4 1.3 gather_fusion
  10.7 0.7 compare_and_fusion
  11.4 49.2 %all-gather.5.cloned.1.call-done = bf16[64,16,512]{2,1,0:T(8,128)(2,1)} async-done(((bf16[4,16,512]{2,1,0:T(8,128)(2,1)}), bf16[64,16,512]{2,1,0:T(8,128)(2,1)}) %all-gather.5.cloned.1.call-update) | async-done | bytes 1048592 | tf_op jit(solution)/shard_map/all_gather | solution.py:34
  60.6 1.8 gather_fusion.1
  62.4 1.0 convolution_bitcast_fusion.1
  63.4 46.7 %all-gather.7.cloned.1.call-done = bf16[64,16,512]{2,1,0:T(8,128)(2,1)} async-done(((bf16[4,16,512]{2,1,0:T(8,128)(2,1)}), bf16[64,16,512]{2,1,0:T(8,128)(2,1)}) %all-gather.7.cloned.1.call-update) | async-done | bytes 1048592 | tf_op jit(solution)/shard_map/all_gather | solution.py:33
  110.1 1.8 gather_fusion.2
  111.8 2.1 convolution_bitcast_fusion
  114.0 0.0 all-reduce.3.cloned.1.call-update
  114.0 0.0 reduce-scatter.6.cloned.1.call-start
  114.0 104.7 %all-reduce.3.cloned.1.call-done = (f32[6,128,16]{1,2,0:T(8,128)}, f32[6,128,16]{1,2,0:T(8,128)}) async-done(((f32[6,128,16]{1,2,0:T(8,128)}, f32[6,128,16]{1,2,0:T(8,128)}), (f32[6,128,16]{1,2,0:T(8,128)}, f32[6,128,16]{1,2,0:T(8,128)})) %all-reduce.3.cloned.1.call-update) | async-done | bytes 98320 | tf_op jit(solution)/shard_map/psum | solution.py:47
  218.8 1.0 convolution_multiply_fusion.2
  219.8 1.1 fusion.2
  220.9 2.5 copy.19
  223.4 0.0 reduce-scatter.6.cloned.1.call-update
  223.5 0.0 reduce-scatter.8.cloned.1.call-start
  223.5 0.7 copy-done.7
  224.2 0.2 convolution_multiply_fusion.1
  224.4 1.1 fusion
  225.6 2.5 copy.21
  228.1 0.0 reduce-scatter.8.cloned.1.call-update
  228.1 0.0 all-gather.9.cloned.1.call-start
  228.2 73.1 %reduce-scatter.6.cloned.1.call-done = f32[4,16,512]{2,1,0:T(8,128)} async-done(((f32[64,16,512]{2,1,0:T(8,128)}), f32[4,16,512]{2,1,0:T(8,128)}) %reduce-scatter.6.cloned.1.call-update) | async-done | bytes 131088 | tf_op jit(solution)/shard_map/reduce_scatter | solution.py:73
  301.2 1.6 subtract_convert_fusion.1
  302.8 0.0 all-gather.9.cloned.1.call-update
  302.8 0.0 all-gather.11.cloned.1.call-start
  302.9 80.5 %reduce-scatter.8.cloned.1.call-done = f32[4,16,512]{2,1,0:T(8,128)} async-done(((f32[64,16,512]{2,1,0:T(8,128)}), f32[4,16,512]{2,1,0:T(8,128)}) %reduce-scatter.8.cloned.1.call-update) | async-done | bytes 131088 | tf_op jit(solution)/shard_map/reduce_scatter | solution.py:74
  383.4 1.6 subtract_convert_fusion
  384.9 0.0 all-gather.11.cloned.1.call-update
  385.0 0.0 reduce-scatter.4.cloned.1.call-start
  385.0 15.2 %fusion.19 = f32[768,8192]{1,0:T(8,128)} fusion(bf16[768,512]{1,0:T(8,128)(2,1)S(1)} %copy-done, bf16[8192,512]{1,0:T(8,128)(2,1)} %param.11), kind=kOutput, calls=%fused_computation.38 | convolution fusion | flops 6442450944 | bytes 34340864 | tf_op jit(solution)/shard_map/dot_general | solution.py:54
  400.2 0.0 reduce-scatter.4.cloned.1.call-update
  400.2 0.8 copy-done.6
  401.0 0.4 convolution_multiply_fusion
  401.4 32.4 %all-gather.9.cloned.1.call-done = bf16[64,16,512]{2,1,0:T(8,128)(2,1)} async-done(((bf16[4,16,512]{2,1,0:T(8,128)(2,1)}), bf16[64,16,512]{2,1,0:T(8,128)(2,1)}) %all-gather.9.cloned.1.call-update) | async-done | bytes 1048592 | tf_op jit(solution)/shard_map/all_gather | solution.py:83
  433.9 50.3 %all-gather.11.cloned.1.call-done = bf16[64,16,512]{2,1,0:T(8,128)(2,1)} async-done(((bf16[4,16,512]{2,1,0:T(8,128)(2,1)}), bf16[64,16,512]{2,1,0:T(8,128)(2,1)}) %all-gather.11.cloned.1.call-update) | async-done | bytes 1048592 | tf_op jit(solution)/shard_map/all_gather | solution.py:84
  484.2 145.3 %reduce-scatter.4.cloned.1.call-done = f32[768,512]{1,0:T(8,128)} async-done(((f32[768,8192]{1,0:T(8,128)}), f32[768,512]{1,0:T(8,128)}) %reduce-scatter.4.cloned.1.call-update) | async-done | bytes 1572880 | tf_op jit(solution)/shard_map/reduce_scatter | solution.py:57
  629.6 2.8 bitcast_add_fusion
  632.3 1.0 copy.30
  633.3 0.6 copy-done.3
  633.9 1.0 copy.31
  (15 shorter events, 0.0 us)
Async XLA Ops:
  7.2 55.2 %copy-start = (bf16[768,512]{1,0:T(8,128)(2,1)S(1)}, bf16[768,512]{1,0:T(8,128)(2,1)}, u32[]{:S(2)}) copy-start(bf16[768,512]{1,0:T(8,128)(2,1)} %param.10) | copy-start | bytes 2359300
  7.2 211.6 %copy-start.1 = (bf16[768,512]{1,0:T(8,128)(2,1)S(1)}, bf16[768,512]{1,0:T(8,128)(2,1)}, u32[]{:S(2)}) copy-start(bf16[768,512]{1,0:T(8,128)(2,1)} %param.9) | copy-start | bytes 2359300
  7.2 53.4 %all-gather.5.cloned.1.call-start = ((), (), s32[]{:S(2)}) async-start(), calls=%async_computation.4 | async-start | bytes 1114112 | tf_op jit(solution)/shard_map/all_gather | solution.py:34
  7.9 102.1 %all-gather.7.cloned.1.call-start = ((), (), s32[]{:S(2)}) async-start(), calls=%async_computation.5 | async-start | bytes 1114112 | tf_op jit(solution)/shard_map/all_gather | solution.py:33
  8.7 210.1 %all-reduce.3.cloned.1.call-start = ((), (), s32[]{:S(2)}) async-start(), calls=%async_computation.10 | async-start | bytes 196608 | tf_op jit(solution)/shard_map/psum | solution.py:47
  114.0 187.2 %reduce-scatter.6.cloned.1.call-start = ((), (), s32[]{:S(2)}) async-start(), calls=%async_computation.6 | async-start | bytes 2228224 | tf_op jit(solution)/shard_map/reduce_scatter | solution.py:73
  223.4 0.8 copy-start.7
  223.5 159.9 %reduce-scatter.8.cloned.1.call-start = ((), (), s32[]{:S(2)}) async-start(), calls=%async_computation.8 | async-start | bytes 2228224 | tf_op jit(solution)/shard_map/reduce_scatter | solution.py:74
  228.1 73.2 %copy-start.4 = (bf16[4,16,512]{2,1,0:T(8,128)(2,1)S(1)}, bf16[4,16,512]{2,1,0:T(8,128)(2,1)}, u32[]{:S(2)}) copy-start(bf16[4,16,512]{2,1,0:T(8,128)(2,1)} %param.12) | copy-start | bytes 196612
  228.1 155.3 %copy-start.5 = (bf16[4,16,512]{2,1,0:T(8,128)(2,1)S(1)}, bf16[4,16,512]{2,1,0:T(8,128)(2,1)}, u32[]{:S(2)}) copy-start(bf16[4,16,512]{2,1,0:T(8,128)(2,1)} %param.13) | copy-start | bytes 196612
  228.1 205.8 %all-gather.9.cloned.1.call-start = ((), (), s32[]{:S(2)}) async-start(), calls=%async_computation.7 | async-start | bytes 1114112 | tf_op jit(solution)/shard_map/all_gather | solution.py:83
  302.8 181.4 %all-gather.11.cloned.1.call-start = ((), (), s32[]{:S(2)}) async-start(), calls=%async_computation.9 | async-start | bytes 1114112 | tf_op jit(solution)/shard_map/all_gather | solution.py:84
  385.0 244.6 %reduce-scatter.4.cloned.1.call-start = ((), (), s32[]{:S(2)}) async-start(), calls=%async_computation.3 | async-start | bytes 26738688 | tf_op jit(solution)/shard_map/reduce_scatter | solution.py:57
  400.2 0.8 copy-start.6
  433.9 198.5 %copy-start.2 = (bf16[64,16,512]{2,1,0:T(8,128)(2,1)S(1)}, bf16[64,16,512]{2,1,0:T(8,128)(2,1)}, u32[]{:S(2)}) copy-start(bf16[64,16,512]{2,1,0:T(8,128)(2,1)} %all-gather.9.cloned.1.call-done) | copy-start | bytes 3145732
  632.3 1.6 copy-start.3
Sparse Core Ops, SparseCore 0:
  10.5 50.0 all-gather.4
  63.0 47.0 all-gather.6
  114.1 104.6 all-reduce.2
  223.6 77.6 reduce-scatter.5
  304.6 78.7 reduce-scatter.7
  386.5 47.2 all-gather.8
  437.2 47.0 all-gather.10
  486.9 142.5 reduce-scatter.3
where the time goes:
time: 643 us; the launch traced here: 642 us
  waiting for transfers between devices  584 us (91%)
  matrix products  22.1 us (3%)
  between operations  14.2 us (2%)
  local copies, waits for them, and re-layouts  14 us (2%)
  other arithmetic  7.22 us (1%)
    reduce_scatter x1, waiting for transfers between devices, shards(): lax.psum_scatter(partial_value, 'tensor', scatter_dimension=1, tiled=True)  145 us
    psum x1, waiting for transfers between devices, shards(): low_sum, back_sum = lax.psum((low_part, back_part), 'tensor')  105 us
    reduce_scatter x1, waiting for transfers between devices, shards(): lax.psum_scatter(up_lookup, 'dp', scatter_dimension=0, tiled=True)  80.5 us
    reduce_scatter x1, waiting for transfers between devices, shards(): lax.psum_scatter(down_lookup, 'dp', scatter_dimension=0, tiled=True)  73.1 us
    all_gather x1, waiting for transfers between devices, shards(): lax.all_gather(stepped_up, 'dp', axis=0, tiled=True)  50.3 us
    all_gather x1, waiting for transfers between devices, shards(): lax.all_gather(up_table_rows, 'dp', axis=0, tiled=True)  49.2 us
    all_gather x1, waiting for transfers between devices, shards(): lax.all_gather(down_table_rows, 'dp', axis=0, tiled=True)  46.7 us
    all_gather x1, waiting for transfers between devices, shards(): lax.all_gather(stepped_down, 'dp', axis=0, tiled=True)  32.4 us
  transfers between devices with their start and end apart: 8, of which 8 were waited for; matrix products, arithmetic and copies ran while one was open for 4% of the time, Pallas kernels for 0%

commit v1 on v0

v1 whole, which is shorter than its diff:
```python
import math

import jax
import jax.numpy as jnp
from jax import lax
from jax.experimental import pallas as pl
from jax.experimental.pallas import tpu as pltpu
from jax.sharding import PartitionSpec as P

MODEL_WIDTH = 8192
RANK = 16
GROUP = 128
ADAPTER_SCALE = 0.25
LEARNING_RATE = 1.5
SCALE_DOWN = 1.0 / math.sqrt(MODEL_WIDTH)
SCALE_UP = ADAPTER_SCALE / math.sqrt(RANK)

SIDE = 4
DEPTH = 8
OWNERS = SIDE * SIDE

POWER_SHIFT = 19.0

MESH = pl.DeviceIdType.MESH
F32 = jnp.float32
BF16 = jnp.bfloat16
I32 = jnp.int32
HOPS = 7
TARGET = ((4, 3, 3, 2, 2, 1, 1), (4, 5, 5, 6, 6, 7, 7))
HALF = ((0, 1, 0, 1, 0, 1, 0), (1, 0, 1, 0, 1, 0, 1))
W_ORDER = (4, 3, 5, 2, 6, 1, 7, 0)


def encode(v):
    u = v * (2.0**POWER_SHIFT)
    return ((u * jnp.abs(u)) * (u * u)).astype(BF16)


def decode(code):
    w = code.astype(F32)
    root = jnp.exp2(jnp.log(jnp.abs(w)) * (0.25 / math.log(2.0)) - POWER_SHIFT)
    return jnp.where(w < 0, -root, root)


class Gather:
    def __init__(self, buf, send, recv, first, second, cut):
        self.buf, self.send, self.recv, self.first, self.second = buf, send, recv, first, second
        rows = buf.shape[1]
        self.parts = {"all": (0, rows), "a": (0, cut), "b": (cut, rows - cut)}
        self.copies = {}

    def go(self, number, device, source, target, part):
        begin, size = self.parts[part]
        copy = pltpu.make_async_remote_copy(
            src_ref=self.buf.at[source, pl.ds(begin, size)],
            dst_ref=self.buf.at[target, pl.ds(begin, size)],
            send_sem=self.send.at[number],
            recv_sem=self.recv.at[number],
            device_id=device,
            device_id_type=MESH,
        )
        copy.start()
        self.copies[number] = copy

    def wait(self, number):
        self.copies[number].wait_recv()

    def start(self):
        self.go(0, self.first(1), 0, 12, "all")
        self.go(1, self.first(-1), 0, 4, "all")

    def across(self, i):
        self.go(4 + 4 * i, self.second(1), 4 * i, 4 * i + 3, "all")
        self.go(5 + 4 * i, self.second(-1), 4 * i, 4 * i + 1, "all")

    def pass_first(self):
        self.wait(0)
        self.go(2, self.first(1), 12, 8, "a")
        self.wait(1)
        self.go(3, self.first(-1), 4, 8, "b")

    def end_first(self):
        self.wait(2)
        self.wait(3)

    def pass_second(self, i):
        self.wait(4 + 4 * i)
        self.go(6 + 4 * i, self.second(1), 4 * i + 3, 4 * i + 2, "a")
        self.wait(5 + 4 * i)
        self.go(7 + 4 * i, self.second(-1), 4 * i + 1, 4 * i + 2, "b")

    def end(self):
        for i in range(SIDE):
            self.wait(6 + 4 * i)
            self.wait(7 + 4 * i)

    def drain(self):
        for copy in self.copies.values():
            copy.wait_send()


def kernel(
    x_hbm,
    dy_hbm,
    w_hbm,
    down_hbm,
    up_hbm,
    adapter,
    slot_of,
    token_out,
    down_out,
    up_out,
    xv,
    dyv,
    wv,
    tab0,
    tab1,
    gr0,
    gr1,
    ids,
    z_in,
    z_out,
    part,
    own,
    rank_own,
    rank_pair,
    rank_chip,
    rank_in,
    rank_all,
    out0,
    out1,
    links_v,
    links_s,
    local_sem,
    pair_send,
    pair_recv,
    t0_send,
    t0_recv,
    t1_send,
    t1_recv,
    g0_send,
    g0_recv,
    g1_send,
    g1_recv,
    z_send,
    z_recv,
    r_send,
    r_recv,
    a_send,
    a_recv,
    i_send,
    i_recv,
):
    dp, tensor = lax.axis_index("dp"), lax.axis_index("tensor")
    x, y = lax.div(dp, SIDE), lax.rem(dp, SIDE)
    z, core = lax.div(tensor, 2), lax.rem(tensor, 2)
    tokens, width = own.shape
    half = tokens // 2
    groups = tokens // GROUP
    mate = (dp, z * 2 + 1 - core)

    def along_x(d):
        return (lax.rem(x + d + SIDE, SIDE) * SIDE + y, tensor)

    def along_y(d):
        return (x * SIDE + lax.rem(y + d + SIDE, SIDE), tensor)

    def chip_z(d):
        return lax.rem(z + d + DEPTH, DEPTH)

    def along_z(d):
        return (dp, chip_z(d) * 2 + core)

    def place0(owner):
        i = lax.rem(lax.div(owner, SIDE) - x + SIDE, SIDE)
        return i * SIDE + lax.rem(lax.rem(owner, SIDE) - y + SIDE, SIDE)

    def place1(owner):
        i = lax.rem(lax.rem(owner, SIDE) - y + SIDE, SIDE)
        return i * SIDE + lax.rem(lax.div(owner, SIDE) - x + SIDE, SIDE)

    def w_rows(rel, parity):
        begin = pl.multiple_of((chip_z(rel) * 2 + parity) * width, width)
        return w_hbm.at[pl.ds(begin, width)]

    loads = [
        pltpu.make_async_copy(down_hbm, tab0.at[0], local_sem.at[0]),
        pltpu.make_async_copy(up_hbm, tab1.at[0], local_sem.at[1]),
        pltpu.make_async_copy(dy_hbm, dyv.at[0], local_sem.at[2]),
        pltpu.make_async_copy(x_hbm, xv, local_sem.at[3]),
    ]
    w_loads = {rel: pltpu.make_async_copy(w_rows(rel, core), wv.at[0, rel], local_sem.at[4 + rel]) for rel in W_ORDER}
    for copy in loads:
        copy.start()
    for rel in W_ORDER:
        w_loads[rel].start()

    row = lax.broadcasted_iota(I32, (8, 128), 0)
    tile = jnp.full((8, 128), -1, I32)
    for g in range(groups):
        tile = jnp.where(row == g, slot_of[adapter[g]], tile)
    ids[dp] = tile

    barrier = pltpu.get_barrier_semaphore()
    pl.semaphore_signal(barrier, inc=1, device_id=mate, device_id_type=MESH)
    for k in range(1, DEPTH):
        pl.semaphore_signal(barrier, inc=1, device_id=along_z(k), device_id_type=MESH)
    for k in range(1, OWNERS):
        pl.semaphore_signal(barrier, inc=1, device_id=(lax.rem(dp + k, OWNERS), tensor), device_id_type=MESH)
    pl.semaphore_wait(barrier, DEPTH + OWNERS - 1)

    def to_mate(source, target, number):
        return pltpu.make_async_remote_copy(
            src_ref=source,
            dst_ref=target,
            send_sem=pair_send.at[number],
            recv_sem=pair_recv.at[number],
            device_id=mate,
            device_id_type=MESH,
        )

    dy_pair = to_mate(dy_hbm, dyv.at[1], 8)
    dy_pair.start()
    w_pair = {rel: to_mate(w_rows(rel, 1 - core), wv.at[1, rel], rel) for rel in W_ORDER}
    w_pair[4].start()

    tables = (
        Gather(tab0, t0_send, t0_recv, along_x, along_y, 2),
        Gather(tab1, t1_send, t1_recv, along_y, along_x, 2),
    )
    loads[0].wait()
    tables[0].start()
    loads[1].wait()
    tables[1].start()
    for table in tables:
        table.across(0)
    for rel in W_ORDER[1:]:
        w_pair[rel].start()

    def frozen(rel, begin, size):
        rows = pl.ds(begin, size)
        dims = (((1,), (1,)), ((), ()))
        first = lax.dot_general(dyv[0, rows], wv[0, rel], dims, preferred_element_type=F32)
        second = lax.dot_general(dyv[1, rows], wv[1, rel], dims, preferred_element_type=F32)
        return first + second

    def z_copy(way, k):
        return pltpu.make_async_remote_copy(
            src_ref=z_out.at[way, k],
            dst_ref=z_in.at[way, k],
            send_sem=z_send.at[way, k],
            recv_sem=z_recv.at[way, k],
            device_id=along_z(1 - 2 * way),
            device_id_type=MESH,
        )

    z_copies = {(way, k): z_copy(way, k) for way in range(2) for k in range(HOPS)}
    strip = 32
    have = set()

    def z_step(k):
        for way in range(2):
            rel = TARGET[way][k]
            if rel not in have:
                have.add(rel)
                w_loads[rel].wait()
                w_pair[rel].wait_recv()
            part[way] = frozen(rel, HALF[way][k] * half, half)
            if k >= 2:
                z_copies[way, k - 2].wait_recv()

            def move(n, carry):
                rows = pl.ds(pl.multiple_of(n * strip, strip), strip)
                v = part[way, rows]
                if k >= 2:
                    v = v + decode(z_in[way, k - 2, rows])
                z_out[way, k, rows] = encode(v)
                return carry

            lax.fori_loop(0, half // strip, move, 0)
            z_copies[way, k].start()

    def z_end(way, k):
        begin = HALF[way][k] * half
        z_copies[way, k].wait_recv()

        def move(n, carry):
            rows = pl.ds(pl.multiple_of(begin + n * strip, strip), strip)
            own[rows] = own[rows] + decode(z_in[way, k, pl.ds(pl.multiple_of(n * strip, strip), strip)])
            return carry

        lax.fori_loop(0, half // strip, move, 0)

    loads[2].wait()
    dy_pair.wait_recv()
    z_step(0)
    for table in tables:
        table.pass_first()
        table.across(3)
        table.across(1)

    def id_copy(k, place):
        return pltpu.make_async_remote_copy(
            src_ref=ids.at[dp],
            dst_ref=ids.at[place],
            send_sem=i_send.at[k],
            recv_sem=i_recv.at[k],
            device_id=(lax.rem(dp + k, OWNERS), tensor),
            device_id_type=MESH,
        )

    for k in range(1, OWNERS):
        id_copy(k, dp).start()
    for table in tables:
        table.end_first()
        table.across(2)
    for i in (0, 3):
        for table in tables:
            table.pass_second(i)
    z_step(1)
    for i in (1, 2):
        for table in tables:
            table.pass_second(i)
    for table in tables:
        table.end()

    loads[3].wait()
    slots = [slot_of[adapter[g]] for g in range(groups)]
    downs, ups = [], []
    for s in slots:
        owner, at = lax.div(s, 4), lax.rem(s, 4)
        downs.append((place0(owner), at))
        ups.append((place1(owner), at))
    for g in range(groups):
        rows = pl.ds(g * GROUP, GROUP)
        dims = (((1,), (1,)), ((), ()))
        low = lax.dot_general(tab0[downs[g]], xv[rows], dims, preferred_element_type=F32)
        back = lax.dot_general(tab1[ups[g]], dyv[0, rows], dims, preferred_element_type=F32)
        rank_own[4 * g : 4 * g + 2] = low.reshape(2, 8, GROUP)
        rank_own[4 * g + 2 : 4 * g + 4] = back.reshape(2, 8, GROUP)
    rank_mate = to_mate(rank_own, rank_pair, 9)
    rank_mate.start()
    rank_mate.wait_recv()
    rank_chip[...] = rank_own[...] + rank_pair[...]
    chunk = rank_own.shape[0] // DEPTH

    def rank_part(d):
        return pl.ds(chip_z(d) * chunk, chunk)

    r_copies, a_copies = [], []
    for k in range(1, DEPTH):
        copy = pltpu.make_async_remote_copy(
            src_ref=rank_chip.at[rank_part(k)],
            dst_ref=rank_in.at[k],
            send_sem=r_send.at[k],
            recv_sem=r_recv.at[k],
            device_id=along_z(k),
            device_id_type=MESH,
        )
        copy.start()
        r_copies.append(copy)
    total = rank_chip[rank_part(0)]
    for k in range(1, DEPTH):
        r_copies[k - 1].wait_recv()
        total = total + rank_in[k]
    rank_all[rank_part(0)] = total

    def a_copy(k, d):
        return pltpu.make_async_remote_copy(
            src_ref=rank_all.at[rank_part(0)],
            dst_ref=rank_all.at[rank_part(d)],
            send_sem=a_send.at[k],
            recv_sem=a_recv.at[k],
            device_id=along_z(k),
            device_id_type=MESH,
        )

    for k in range(1, DEPTH):
        copy = a_copy(k, 0)
        copy.start()
        a_copies.append(copy)
    z_step(2)
    for k in range(1, DEPTH):
        a_copy(k, -k).wait_recv()

    def low_of(g):
        return (rank_all[4 * g : 4 * g + 2].reshape(RANK, GROUP) * SCALE_DOWN).astype(BF16)

    def back_of(g):
        return (rank_all[4 * g + 2 : 4 * g + 4].reshape(RANK, GROUP) * SCALE_UP).astype(BF16)

    for g in range(groups):
        rows = pl.ds(g * GROUP, GROUP)
        gr0[0, g] = jnp.dot(back_of(g), xv[rows], preferred_element_type=F32) * SCALE_DOWN
        gr1[0, g] = jnp.dot(low_of(g), dyv[0, rows], preferred_element_type=F32) * SCALE_UP
    grads = (
        Gather(gr0, g0_send, g0_recv, along_x, along_y, groups // 2),
        Gather(gr1, g1_send, g1_recv, along_y, along_x, groups // 2),
    )
    for grad in grads:
        grad.start()
    for grad in grads:
        grad.across(0)
    z_step(3)

    have.add(0)
    w_loads[0].wait()
    w_pair[0].wait_recv()
    for g in range(groups):
        rows = pl.ds(g * GROUP, GROUP)
        term = lax.dot_general(back_of(g), tab0[downs[g]], (((0,), (0,)), ((), ())), preferred_element_type=F32)
        own[rows] = frozen(0, g * GROUP, GROUP) + term * SCALE_DOWN

    for k in range(1, OWNERS):
        id_copy(k, lax.rem(dp - k + OWNERS, OWNERS)).wait_recv()
    by_row = ids[...].reshape(OWNERS * 8, 128)
    by_column = by_row.T
    row = lax.broadcasted_iota(I32, by_row.shape, 0)
    column = lax.broadcasted_iota(I32, by_row.shape, 1)
    before = jnp.where((by_row == by_column) & (row < column), row, -1)
    last = jnp.where(by_row == column, row, -1)
    links_v[0:1] = jnp.max(before, axis=0, keepdims=True)
    links_v[1:2] = jnp.max(last, axis=0, keepdims=True)
    links = pltpu.make_async_copy(links_v, links_s, local_sem.at[12])
    links.start()

    for grad in grads:
        grad.pass_first()
        grad.across(3)
        grad.across(1)
    z_step(4)
    for grad in grads:
        grad.pass_second(0)
    for grad in grads:
        grad.end_first()
        grad.across(2)
    z_step(5)
    for grad in grads:
        grad.pass_second(3)
    for grad in grads:
        grad.pass_second(1)
    z_step(6)
    for grad in grads:
        grad.pass_second(2)
    for way in range(2):
        z_end(way, 5)
    for grad in grads:
        grad.end()
    for grad in grads:
        grad.drain()
    links.wait()

    def add_owner(d, carry):
        for g in range(groups):
            link = links_s[0, d * 8 + g]
            keep = jnp.where(link >= 0, 1.0, 0.0).astype(F32)
            link = jnp.maximum(link, 0)
            owner, at = lax.div(link, 8), lax.rem(link, 8)
            here = place0(d)
            gr0[here, g] = gr0[here, g] + keep * gr0[place0(owner), at]
            here = place1(d)
            gr1[here, g] = gr1[here, g] + keep * gr1[place1(owner), at]
        return carry

    lax.fori_loop(0, OWNERS, add_owner, 0)

    def step_slot(s, carry):
        link = links_s[1, s]
        keep = jnp.where(link >= 0, LEARNING_RATE, 0.0).astype(F32)
        link = jnp.maximum(link, 0)
        owner, at = lax.div(link, 8), lax.rem(link, 8)
        home, spot = lax.div(s, 4), lax.rem(s, 4)
        out0[s] = (tab0[place0(home), spot].astype(F32) - keep * gr0[place0(owner), at]).astype(BF16)
        out1[s] = (tab1[place1(home), spot].astype(F32) - keep * gr1[place1(owner), at]).astype(BF16)
        return carry

    lax.fori_loop(0, out0.shape[0], step_slot, 0)
    stores = [
        pltpu.make_async_copy(out0, down_out, local_sem.at[13]),
        pltpu.make_async_copy(out1, up_out, local_sem.at[14]),
    ]
    for copy in stores:
        copy.start()

    for way in range(2):
        z_end(way, 6)
        rows = pl.ds(HALF[way][6] * half, half)
        copy = pltpu.make_async_copy(own.at[rows], token_out.at[rows], local_sem.at[15 + way])
        copy.start()
        stores.append(copy)

    for copy in [dy_pair, rank_mate, *w_pair.values(), *z_copies.values(), *r_copies, *a_copies]:
        copy.wait_send()
    for k in range(1, OWNERS):
        id_copy(k, dp).wait_send()
    for table in tables:
        table.drain()
    for copy in stores:
        copy.wait()


def shards(x, dy, w, down, up, adapter, slot_of):
    tokens, width = x.shape
    owned, rank, _ = down.shape
    groups = adapter.shape[0]
    slots = owned * OWNERS
    tiles = groups * 4
    any_space = pl.BlockSpec(memory_space=pl.ANY)
    smem = pl.BlockSpec(memory_space=pltpu.SMEM)
    dma = pltpu.SemaphoreType.DMA
    vmem = pltpu.VMEM
    return pl.pallas_call(
        kernel,
        out_shape=(
            jax.ShapeDtypeStruct((tokens, width), F32),
            jax.ShapeDtypeStruct((slots, rank, width), BF16),
            jax.ShapeDtypeStruct((slots, rank, width), BF16),
        ),
        in_specs=[any_space] * 5 + [smem] * 2,
        out_specs=(any_space,) * 3,
        scratch_shapes=[
            vmem((tokens, width), BF16),
            vmem((2, tokens, width), BF16),
            vmem((2, DEPTH, width, width), BF16),
            vmem((OWNERS, owned, rank, width), BF16),
            vmem((OWNERS, owned, rank, width), BF16),
            vmem((OWNERS, groups, rank, width), F32),
            vmem((OWNERS, groups, rank, width), F32),
            vmem((OWNERS, 8, 128), I32),
            vmem((2, HOPS, tokens // 2, width), BF16),
            vmem((2, HOPS, tokens // 2, width), BF16),
            vmem((2, tokens // 2, width), F32),
            vmem((tokens, width), F32),
            vmem((tiles, 8, GROUP), F32),
            vmem((tiles, 8, GROUP), F32),
            vmem((tiles, 8, GROUP), F32),
            vmem((DEPTH, tiles // DEPTH, 8, GROUP), F32),
            vmem((tiles, 8, GROUP), F32),
            vmem((slots, rank, width), BF16),
            vmem((slots, rank, width), BF16),
            vmem((8, 128), I32),
            pltpu.SMEM((8, 128), I32),
            dma((17,)),
            dma((10,)),
            dma((10,)),
        ]
        + [dma((20,))] * 8
        + [dma((2, HOPS))] * 2
        + [dma((DEPTH,))] * 4
        + [dma((OWNERS,))] * 2,
        compiler_params=pltpu.CompilerParams(
            collective_id=0, has_side_effects=True, vmem_limit_bytes=56 * 1024 * 1024
        ),
        name="lora_step",
    )(x, dy, w, down, up, adapter, slot_of)


def solution(mesh):
    return jax.shard_map(
        shards,
        mesh=mesh,
        in_specs=(
            P("dp", "tensor"),
            P("dp", "tensor"),
            P(None, "tensor"),
            P("dp", None, "tensor"),
            P("dp", None, "tensor"),
            P("dp"),
            P(),
        ),
        out_specs=(P("dp", "tensor"), P(None, None, "tensor"), P(None, None, "tensor")),
        check_vma=False,
    )
```

time: 643 us -> 93.8 us (0.15)
  waiting for transfers between devices: 584 us -> 0 us
  Pallas kernels: 0 us -> 86.2 us
  matrix products: 22.1 us -> 0 us
  between operations: 14.2 us -> 0.65 us
  local copies, waits for them, and re-layouts: 14 us -> 5.33 us
  other arithmetic: 7.22 us -> 0 us
    reduce_scatter x3 -> x0, waiting for transfers between devices: 299 us -> none  [the longest x1 145 us: shards(): lax.psum_scatter(partial_value, 'tensor', scatter_dimension=1, tiled=True)]
    all_gather x4 -> x0, waiting for transfers between devices: 179 us -> none  [the longest x1 50.3 us: shards(): lax.all_gather(stepped_up, 'dp', axis=0, tiled=True)]
    psum x1 -> x0, waiting for transfers between devices: 105 us -> none  [shards(): low_sum, back_sum = lax.psum((low_part, back_part), 'tensor')]
    pallas_call x0 -> x1, Pallas kernels: none -> 86.2 us  [shards(): pl.pallas_call(kernel, out_shape=(jax.ShapeDtypeStruct((tokens, width), F...]
    dot_general x8 -> x0, matrix products: 22.1 us -> none  [the longest x1 15.2 us: shards(): lax.dot_general(query_gradient, query_matrix, (((1,), (1,)), ((), ())), p...]
  transfers between devices with their start and end apart: 8 -> 0, of which waited for: 8 -> 0; matrix products, arithmetic and copies ran while one was open for 4% -> 0% of each run, Pallas kernels for 0% -> 0%
where the time goes in v1:
time: 93.8 us; the launch traced here: 92.2 us
  Pallas kernels  86.2 us (92%)
  local copies, waits for them, and re-layouts  5.33 us (6%)
    pallas_call x1, Pallas kernels, shards(): pl.pallas_call(kernel, out_shape=(jax.ShapeDtypeStruct((tokens, width), F...  86.2 us
    unnamed x7, local copies, waits for them, and re-layouts  5.33 us

profile of v1, /device:TPU:1, one launch (start us, length us, event | category | flops | bytes accessed | tf_op | source)
XLA Modules:
  0.0 92.2 jit_solution(13954729938144104317)
XLA Ops:
  0.6 86.2 %lora_step.1 = (f32[768,512]{1,0:T(8,128)}, bf16[64,16,512]{2,1,0:T(8,128)(2,1)}, bf16[64,16,512]{2,1,0:T(8,128)(2,1)}) custom-call(bf16[768,512]{1,0:T(8,128)(2,1)} %x_hbm.1, bf16[768,512]{1,0:T(8,128)(2,1)} %dy_hbm.1, bf16[8192,512]{1,0:T(8,128)(2,1)} %w_hbm.1, bf16[4,16,512]{2,1,0:T(8,128)(2,1)} %down_hbm.1, bf16[4,16,512]{2,1,0:T(8,128)(2,1)} %up_hbm.1, ...), custom_call_target="tpu_custom_call" | custom-call | tf_op jit(solution)/shard_map/lora_step/pallas_call | solution.py:512
  86.9 0.0 copy-start.1
  86.9 2.8 %copy.13 = f32[768,512]{1,0:T(8,128)} copy(f32[768,512]{1,0:T(8,128)} %get-tuple-element.6) | data formatting | bytes 3145728
  89.6 0.0 copy-done.1
  89.6 0.0 copy-start
  89.6 1.0 %copy.14 = bf16[64,16,512]{2,1,0:T(8,128)(2,1)} copy(bf16[64,16,512]{2,1,0:T(8,128)(2,1)S(1)} %copy-done.1) | data formatting | bytes 2097152
  90.6 0.6 copy-done
  91.2 1.0 %copy.15 = bf16[64,16,512]{2,1,0:T(8,128)(2,1)} copy(bf16[64,16,512]{2,1,0:T(8,128)(2,1)S(1)} %copy-done) | data formatting | bytes 2097152
Async XLA Ops:
  86.9 2.8 %copy-start.1 = (bf16[64,16,512]{2,1,0:T(8,128)(2,1)S(1)}, bf16[64,16,512]{2,1,0:T(8,128)(2,1)}, u32[]{:S(2)}) copy-start(bf16[64,16,512]{2,1,0:T(8,128)(2,1)} %get-tuple-element.7) | copy-start | bytes 3145732
  89.6 1.6 %copy-start = (bf16[64,16,512]{2,1,0:T(8,128)(2,1)S(1)}, bf16[64,16,512]{2,1,0:T(8,128)(2,1)}, u32[]{:S(2)}) copy-start(bf16[64,16,512]{2,1,0:T(8,128)(2,1)} %get-tuple-element.8) | copy-start | bytes 3145732

commit v2 on v1

--- a/solution.py
+++ b/solution.py
@@ -40,6 +40,23 @@
     w = code.astype(F32)
     root = jnp.exp2(jnp.log(jnp.abs(w)) * (0.25 / math.log(2.0)) - POWER_SHIFT)
     return jnp.where(w < 0, -root, root)
+
+
+BLOCK_SHIFT = 7.8
+
+
+def encode_block(v):
+    most = jnp.maximum(jnp.max(jnp.max(jnp.abs(v), axis=0, keepdims=True), axis=1, keepdims=True), 1e-30)
+    u = v * (2.0**BLOCK_SHIFT / most)
+    u2 = u * u
+    u4 = u2 * u2
+    return (((u4 * u4) * u4) * (u2 * (u * jnp.abs(u)))).astype(BF16), most
+
+
+def decode_block(code, most):
+    w = code.astype(F32)
+    root = jnp.exp2(jnp.log(jnp.abs(w)) * (0.0625 / math.log(2.0)) - BLOCK_SHIFT)
+    return jnp.where(w < 0, -root, root) * jnp.concatenate([most] * (w.shape[1] // 128), axis=1)
 
 
 class Gather:
@@ -107,7 +124,8 @@
     up_hbm,
     adapter,
     slot_of,
-    token_out,
+    own_out,
+    last_out,
     down_out,
     up_out,
     xv,
@@ -115,8 +133,11 @@
     wv,
     tab0,
     tab1,
-    gr0,
-    gr1,
+    code0,
+    code1,
+    most,
+    sum0,
+    sum1,
     ids,
     z_in,
     z_out,
@@ -150,6 +171,8 @@
     a_recv,
     i_send,
     i_recv,
+    m_send,
+    m_recv,
 ):
     dp, tensor = lax.axis_index("dp"), lax.axis_index("tensor")
     x, y = lax.div(dp, SIDE), lax.rem(dp, SIDE)
@@ -190,9 +213,12 @@
         pltpu.make_async_copy(x_hbm, xv, local_sem.at[3]),
     ]
     w_loads = {rel: pltpu.make_async_copy(w_rows(rel, core), wv.at[0, rel], local_sem.at[4 + rel]) for rel in W_ORDER}
-    for copy in loads:
-        copy.start()
-    for rel in W_ORDER:
+    w_loads[4].start()
+    loads[2].start()
+    loads[0].start()
+    loads[1].start()
+    loads[3].start()
+    for rel in W_ORDER[1:]:
         w_loads[rel].start()
 
     row = lax.broadcasted_iota(I32, (8, 128), 0)
@@ -219,10 +245,21 @@
             device_id_type=MESH,
         )
 
-    dy_pair = to_mate(dy_hbm, dyv.at[1], 8)
-    dy_pair.start()
     w_pair = {rel: to_mate(w_rows(rel, 1 - core), wv.at[1, rel], rel) for rel in W_ORDER}
-    w_pair[4].start()
+
+    def send_w(rel):
+        begin = (chip_z(rel) * 2 + 1 - core) * width
+        for n in range(0, width, GROUP):
+            source = w_hbm.at[pl.ds(pl.multiple_of(begin + n, GROUP), GROUP)]
+            to_mate(source, wv.at[1, rel, pl.ds(n, GROUP)], rel).start()
+
+    send_w(4)
+    dy_pair = {}
+    for c in range(half // GROUP):
+        for begin in (c * GROUP, half + c * GROUP):
+            rows = pl.ds(begin, GROUP)
+            dy_pair[begin] = to_mate(dy_hbm.at[rows], dyv.at[1, rows], 10 + begin // GROUP)
+            dy_pair[begin].start()
 
     tables = (
         Gather(tab0, t0_send, t0_recv, along_x, along_y, 2),
@@ -234,8 +271,8 @@
     tables[1].start()
     for table in tables:
         table.across(0)
-    for rel in W_ORDER[1:]:
-        w_pair[rel].start()
+    send_w(3)
+    send_w(5)
 
     def frozen(rel, begin, size):
         rows = pl.ds(begin, size)
@@ -244,10 +281,10 @@
         second = lax.dot_general(dyv[1, rows], wv[1, rel], dims, preferred_element_type=F32)
         return first + second
 
-    def z_copy(way, k):
+    def z_copy(way, k, rows=pl.ds(0, half)):
         return pltpu.make_async_remote_copy(
-            src_ref=z_out.at[way, k],
-            dst_ref=z_in.at[way, k],
+            src_ref=z_out.at[way, k, rows],
+            dst_ref=z_in.at[way, k, rows] if k < HOPS - 1 else last_out.at[way, rows],
             send_sem=z_send.at[way, k],
             recv_sem=z_recv.at[way, k],
             device_id=along_z(1 - 2 * way),
@@ -255,7 +292,7 @@
         )
 
     z_copies = {(way, k): z_copy(way, k) for way in range(2) for k in range(HOPS)}
-    strip = 32
+    strip = 64
     have = set()
 
     def z_step(k):
@@ -275,10 +312,10 @@
                 if k >= 2:
                     v = v + decode(z_in[way, k - 2, rows])
                 z_out[way, k, rows] = encode(v)
+                z_copy(way, k, rows).start()
                 return carry
 
             lax.fori_loop(0, half // strip, move, 0)
-            z_copies[way, k].start()
 
     def z_end(way, k):
         begin = HALF[way][k] * half
@@ -292,8 +329,17 @@
         lax.fori_loop(0, half // strip, move, 0)
 
     loads[2].wait()
-    dy_pair.wait_recv()
-    z_step(0)
+    w_loads[4].wait()
+    w_pair[4].wait_recv()
+    have.add(4)
+    for c in range(half // GROUP):
+        for way in range(2):
+            begin = HALF[way][0] * half + c * GROUP
+            dy_pair[begin].wait_recv()
+            rows = pl.ds(c * GROUP, GROUP)
+            z_out[way, 0, rows] = encode(frozen(4, begin, GROUP))
+            for n in range(GROUP // strip):
+                z_copy(way, 0, pl.ds(c * GROUP + n * strip, strip)).start()
     for table in tables:
         table.pass_first()
         table.across(3)
@@ -311,18 +357,27 @@
 
     for k in range(1, OWNERS):
         id_copy(k, dp).start()
+    z_step(1)
+    for rel in (2, 6, 0):
+        send_w(rel)
     for table in tables:
         table.end_first()
         table.across(2)
     for i in (0, 3):
         for table in tables:
             table.pass_second(i)
-    z_step(1)
+    z_step(2)
     for i in (1, 2):
         for table in tables:
             table.pass_second(i)
+    w_loads[0].wait()
+    w_pair[0].wait_recv()
+    for way in range(2):
+        own[pl.ds(way * half, half)] = frozen(0, way * half, half)
     for table in tables:
         table.end()
+    for rel in (1, 7):
+        send_w(rel)
 
     loads[3].wait()
     slots = [slot_of[adapter[g]] for g in range(groups)]
@@ -336,21 +391,17 @@
         dims = (((1,), (1,)), ((), ()))
         low = lax.dot_general(tab0[downs[g]], xv[rows], dims, preferred_element_type=F32)
         back = lax.dot_general(tab1[ups[g]], dyv[0, rows], dims, preferred_element_type=F32)
-        rank_own[4 * g : 4 * g + 2] = low.reshape(2, 8, GROUP)
-        rank_own[4 * g + 2 : 4 * g + 4] = back.reshape(2, 8, GROUP)
-    rank_mate = to_mate(rank_own, rank_pair, 9)
+        rank_own[0, g] = low
+        rank_own[1, g] = back
+    rank_mate = to_mate(rank_own.at[1 - core], rank_pair, 8)
     rank_mate.start()
     rank_mate.wait_recv()
-    rank_chip[...] = rank_own[...] + rank_pair[...]
-    chunk = rank_own.shape[0] // DEPTH
-
-    def rank_part(d):
-        return pl.ds(chip_z(d) * chunk, chunk)
-
-    r_copies, a_copies = [], []
+    rank_chip[...] = rank_own[core] + rank_pair[...]
+
+    r_copies = []
     for k in range(1, DEPTH):
         copy = pltpu.make_async_remote_copy(
-            src_ref=rank_chip.at[rank_part(k)],
+            src_ref=rank_chip.at[lax.rem(chip_z(k), groups)],
             dst_ref=rank_in.at[k],
             send_sem=r_send.at[k],
             recv_sem=r_recv.at[k],
@@ -359,58 +410,26 @@
         )
         copy.start()
         r_copies.append(copy)
-    total = rank_chip[rank_part(0)]
+    z_step(3)
+    total = rank_chip[lax.rem(z, groups)]
     for k in range(1, DEPTH):
         r_copies[k - 1].wait_recv()
         total = total + rank_in[k]
-    rank_all[rank_part(0)] = total
+    rank_all[core, z] = (total * jnp.where(core == 0, SCALE_DOWN, SCALE_UP).astype(F32)).astype(BF16)
 
     def a_copy(k, d):
         return pltpu.make_async_remote_copy(
-            src_ref=rank_all.at[rank_part(0)],
-            dst_ref=rank_all.at[rank_part(d)],
+            src_ref=rank_all.at[core, z],
+            dst_ref=rank_all.at[core, chip_z(d)],
             send_sem=a_send.at[k],
             recv_sem=a_recv.at[k],
             device_id=along_z(k),
             device_id_type=MESH,
         )
 
-    for k in range(1, DEPTH):
-        copy = a_copy(k, 0)
+    a_copies = [a_copy(k, 0) for k in range(1, DEPTH)]
+    for copy in a_copies:
         copy.start()
-        a_copies.append(copy)
-    z_step(2)
-    for k in range(1, DEPTH):
-        a_copy(k, -k).wait_recv()
-
-    def low_of(g):
-        return (rank_all[4 * g : 4 * g + 2].reshape(RANK, GROUP) * SCALE_DOWN).astype(BF16)
-
-    def back_of(g):
-        return (rank_all[4 * g + 2 : 4 * g + 4].reshape(RANK, GROUP) * SCALE_UP).astype(BF16)
-
-    for g in range(groups):
-        rows = pl.ds(g * GROUP, GROUP)
-        gr0[0, g] = jnp.dot(back_of(g), xv[rows], preferred_element_type=F32) * SCALE_DOWN
-        gr1[0, g] = jnp.dot(low_of(g), dyv[0, rows], preferred_element_type=F32) * SCALE_UP
-    grads = (
-        Gather(gr0, g0_send, g0_recv, along_x, along_y, groups // 2),
-        Gather(gr1, g1_send, g1_recv, along_y, along_x, groups // 2),
-    )
-    for grad in grads:
-        grad.start()
-    for grad in grads:
-        grad.across(0)
-    z_step(3)
-
-    have.add(0)
-    w_loads[0].wait()
-    w_pair[0].wait_recv()
-    for g in range(groups):
-        rows = pl.ds(g * GROUP, GROUP)
-        term = lax.dot_general(back_of(g), tab0[downs[g]], (((0,), (0,)), ((), ())), preferred_element_type=F32)
-        own[rows] = frozen(0, g * GROUP, GROUP) + term * SCALE_DOWN
-
     for k in range(1, OWNERS):
         id_copy(k, lax.rem(dp - k + OWNERS, OWNERS)).wait_recv()
     by_row = ids[...].reshape(OWNERS * 8, 128)
@@ -424,30 +443,77 @@
     links = pltpu.make_async_copy(links_v, links_s, local_sem.at[12])
     links.start()
 
+    for k in range(1, DEPTH):
+        a_copy(k, -k).wait_recv()
+    halves_out = to_mate(rank_all.at[core], rank_all.at[core], 9)
+    halves_out.start()
+    z_step(4)
+    to_mate(rank_all.at[core], rank_all.at[1 - core], 9).wait_recv()
+
+    def low_of(g):
+        return rank_all[0, g]
+
+    def back_of(g):
+        return rank_all[1, g]
+
+    row = lax.broadcasted_iota(I32, (8, 128), 0)
+    most0, most1 = jnp.zeros((8, 128), F32), jnp.zeros((8, 128), F32)
+    for g in range(groups):
+        rows = pl.ds(g * GROUP, GROUP)
+        code, high = encode_block(jnp.dot(back_of(g), xv[rows], preferred_element_type=F32) * SCALE_DOWN)
+        code0[0, g] = code
+        most0 = jnp.where(row == g, high, most0)
+        code, high = encode_block(jnp.dot(low_of(g), dyv[0, rows], preferred_element_type=F32) * SCALE_UP)
+        code1[0, g] = code
+        most1 = jnp.where(row == g, high, most1)
+    most[dp, 0:8] = most0
+    most[dp, 8:16] = most1
+    grads = (
+        Gather(code0, g0_send, g0_recv, along_x, along_y, groups // 2),
+        Gather(code1, g1_send, g1_recv, along_y, along_x, groups // 2),
+    )
+    for grad in grads:
+        grad.start()
+    for grad in grads:
+        grad.across(0)
+
+    def most_copy(k, place):
+        return pltpu.make_async_remote_copy(
+            src_ref=most.at[dp],
+            dst_ref=most.at[place],
+            send_sem=m_send.at[k],
+            recv_sem=m_recv.at[k],
+            device_id=(lax.rem(dp + k, OWNERS), tensor),
+            device_id_type=MESH,
+        )
+
+    for k in range(1, OWNERS):
+        most_copy(k, dp).start()
+    for g in range(groups):
+        rows = pl.ds(g * GROUP, GROUP)
+        term = lax.dot_general(back_of(g), tab0[downs[g]], (((0,), (0,)), ((), ())), preferred_element_type=F32)
+        own[rows] = own[rows] + term * SCALE_DOWN
+
+    z_step(5)
     for grad in grads:
         grad.pass_first()
         grad.across(3)
         grad.across(1)
-    z_step(4)
     for grad in grads:
         grad.pass_second(0)
     for grad in grads:
         grad.end_first()
         grad.across(2)
-    z_step(5)
-    for grad in grads:
-        grad.pass_second(3)
-    for grad in grads:
-        grad.pass_second(1)
+    for i in (3, 1):
+        for grad in grads:
+            grad.pass_second(i)
     z_step(6)
     for grad in grads:
         grad.pass_second(2)
-    for way in range(2):
-        z_end(way, 5)
     for grad in grads:
         grad.end()
-    for grad in grads:
-        grad.drain()
+    for k in range(1, OWNERS):
+        most_copy(k, lax.rem(dp - k + OWNERS, OWNERS)).wait_recv()
     links.wait()
 
     def add_owner(d, carry):
@@ -456,12 +522,12 @@
             keep = jnp.where(link >= 0, 1.0, 0.0).astype(F32)
             link = jnp.maximum(link, 0)
             owner, at = lax.div(link, 8), lax.rem(link, 8)
-            here = place0(d)
-            gr0[here, g] = gr0[here, g] + keep * gr0[place0(owner), at]
-            here = place1(d)
-            gr1[here, g] = gr1[here, g] + keep * gr1[place1(owner), at]
+            sum0[d, g] = decode_block(code0[place0(d), g], most[d, g : g + 1]) + keep * sum0[owner, at]
+            sum1[d, g] = decode_block(code1[place1(d), g], most[d, 8 + g : 9 + g]) + keep * sum1[owner, at]
         return carry
 
+    sum0[0, 0] = jnp.zeros(sum0.shape[2:], F32)
+    sum1[0, 0] = jnp.zeros(sum1.shape[2:], F32)
     lax.fori_loop(0, OWNERS, add_owner, 0)
 
     def step_slot(s, carry):
@@ -470,8 +536,8 @@
         link = jnp.maximum(link, 0)
         owner, at = lax.div(link, 8), lax.rem(link, 8)
         home, spot = lax.div(s, 4), lax.rem(s, 4)
-        out0[s] = (tab0[place0(home), spot].astype(F32) - keep * gr0[place0(owner), at]).astype(BF16)
-        out1[s] = (tab1[place1(home), spot].astype(F32) - keep * gr1[place1(owner), at]).astype(BF16)
+        out0[s] = (tab0[place0(home), spot].astype(F32) - keep * sum0[owner, at]).astype(BF16)
+        out1[s] = (tab1[place1(home), spot].astype(F32) - keep * sum1[owner, at]).astype(BF16)
         return carry
 
     lax.fori_loop(0, out0.shape[0], step_slot, 0)
@@ -481,22 +547,82 @@
     ]
     for copy in stores:
         copy.start()
-
     for way in range(2):
-        z_end(way, 6)
-        rows = pl.ds(HALF[way][6] * half, half)
-        copy = pltpu.make_async_copy(own.at[rows], token_out.at[rows], local_sem.at[15 + way])
-        copy.start()
-        stores.append(copy)
-
-    for copy in [dy_pair, rank_mate, *w_pair.values(), *z_copies.values(), *r_copies, *a_copies]:
+        z_end(way, 5)
+    stores.append(pltpu.make_async_copy(own, own_out, local_sem.at[15]))
+    stores[-1].start()
+    for way in range(2):
+        z_copies[way, HOPS - 1].wait_recv()
+    for copy in [*dy_pair.values(), rank_mate, halves_out, *w_pair.values(), *z_copies.values(), *r_copies, *a_copies]:
         copy.wait_send()
     for k in range(1, OWNERS):
         id_copy(k, dp).wait_send()
-    for table in tables:
-        table.drain()
+        most_copy(k, dp).wait_send()
+    for gather in [*tables, *grads]:
+        gather.drain()
     for copy in stores:
         copy.wait()
+
+
+PIECES = 6
+COPIES = 4
+
+
+def finish_kernel(own_in, last_in, down_in, up_in, token_out, down_out, up_out, own, last, down, up, load_sem, store_sem):
+    def pieces(array, count):
+        size = array.shape[0] // count
+        return [pl.ds(c * size, size) for c in range(count)]
+
+    def load(j, source, target, count):
+        copies = [
+            pltpu.make_async_copy(source.at[rows], target.at[rows], load_sem.at[j, c])
+            for c, rows in enumerate(pieces(target, count))
+        ]
+        for copy in copies:
+            copy.start()
+        return copies
+
+    stores = []
+
+    def store(j, c, source, target, rows):
+        copy = pltpu.make_async_copy(source.at[rows], target.at[rows], store_sem.at[j, c])
+        copy.start()
+        stores.append(copy)
+
+    tables = [(load(2, down_in, down, COPIES), down, down_out), (load(3, up_in, up, COPIES), up, up_out)]
+    own_loads, last_loads = load(0, own_in, own, PIECES), load(1, last_in, last, PIECES)
+    for j, (loads, held, target) in enumerate(tables):
+        for c, rows in enumerate(pieces(held, COPIES)):
+            loads[c].wait()
+            store(1 + j, c, held, target, rows)
+    for c, rows in enumerate(pieces(own, PIECES)):
+        own_loads[c].wait()
+        last_loads[c].wait()
+        own[rows] = own[rows] + decode(last[rows])
+        store(0, c, own, token_out, rows)
+    for copy in stores:
+        copy.wait()
+
+
+def finish(own, last, down, up):
+    any_space = pl.BlockSpec(memory_space=pl.ANY)
+    dma = pltpu.SemaphoreType.DMA
+    return pl.pallas_call(
+        finish_kernel,
+        out_shape=tuple(jax.ShapeDtypeStruct(a.shape, a.dtype) for a in (own, down, up)),
+        in_specs=[any_space] * 4,
+        out_specs=(any_space,) * 3,
+        scratch_shapes=[
+            pltpu.VMEM(own.shape, F32),
+            pltpu.VMEM(last.shape, BF16),
+            pltpu.VMEM(down.shape, BF16),
+            pltpu.VMEM(up.shape, BF16),
+            dma((4, PIECES)),
+            dma((3, PIECES)),
+        ],
+        compiler_params=pltpu.CompilerParams(vmem_limit_bytes=56 * 1024 * 1024),
+        name="finish",
+    )(own, last, down, up)
 
 
 def shards(x, dy, w, down, up, adapter, slot_of):
@@ -504,26 +630,29 @@
     owned, rank, _ = down.shape
     groups = adapter.shape[0]
     slots = owned * OWNERS
-    tiles = groups * 4
     any_space = pl.BlockSpec(memory_space=pl.ANY)
     smem = pl.BlockSpec(memory_space=pltpu.SMEM)
     dma = pltpu.SemaphoreType.DMA
     vmem = pltpu.VMEM
-    return pl.pallas_call(
+    own, last, stepped_down, stepped_up = pl.pallas_call(
         kernel,
         out_shape=(
             jax.ShapeDtypeStruct((tokens, width), F32),
+            jax.ShapeDtypeStruct((2, tokens // 2, width), BF16),
             jax.ShapeDtypeStruct((slots, rank, width), BF16),
             jax.ShapeDtypeStruct((slots, rank, width), BF16),
         ),
         in_specs=[any_space] * 5 + [smem] * 2,
-        out_specs=(any_space,) * 3,
+        out_specs=(any_space,) * 4,
         scratch_shapes=[
             vmem((tokens, width), BF16),
             vmem((2, tokens, width), BF16),
             vmem((2, DEPTH, width, width), BF16),
             vmem((OWNERS, owned, rank, width), BF16),
             vmem((OWNERS, owned, rank, width), BF16),
+            vmem((OWNERS, groups, rank, width), BF16),
+            vmem((OWNERS, groups, rank, width), BF16),
+            vmem((OWNERS, 16, 128), F32),
             vmem((OWNERS, groups, rank, width), F32),
             vmem((OWNERS, groups, rank, width), F32),
             vmem((OWNERS, 8, 128), I32),
@@ -531,28 +660,29 @@
             vmem((2, HOPS, tokens // 2, width), BF16),
             vmem((2, tokens // 2, width), F32),
             vmem((tokens, width), F32),
-            vmem((tiles, 8, GROUP), F32),
-            vmem((tiles, 8, GROUP), F32),
-            vmem((tiles, 8, GROUP), F32),
-            vmem((DEPTH, tiles // DEPTH, 8, GROUP), F32),
-            vmem((tiles, 8, GROUP), F32),
+            vmem((2, groups, RANK, GROUP), F32),
+            vmem((groups, RANK, GROUP), F32),
+            vmem((groups, RANK, GROUP), F32),
+            vmem((DEPTH, RANK, GROUP), F32),
+            vmem((2, DEPTH, RANK, GROUP), BF16),
             vmem((slots, rank, width), BF16),
             vmem((slots, rank, width), BF16),
             vmem((8, 128), I32),
             pltpu.SMEM((8, 128), I32),
-            dma((17,)),
-            dma((10,)),
-            dma((10,)),
+            dma((16,)),
+            dma((10 + groups,)),
+            dma((10 + groups,)),
         ]
         + [dma((20,))] * 8
         + [dma((2, HOPS))] * 2
         + [dma((DEPTH,))] * 4
-        + [dma((OWNERS,))] * 2,
+        + [dma((OWNERS,))] * 4,
         compiler_params=pltpu.CompilerParams(
             collective_id=0, has_side_effects=True, vmem_limit_bytes=56 * 1024 * 1024
         ),
         name="lora_step",
     )(x, dy, w, down, up, adapter, slot_of)
+    return finish(own, last.reshape(tokens, width), stepped_down, stepped_up)
 
 
 def solution(mesh):

time: 93.8 us -> 90.8 us (0.968); the launches traced: 92.2 us -> 90.7 us
  local copies, waits for them, and re-layouts: 5.33 us -> 0 us
  Pallas kernels: 86.2 us -> 90.1 us
    unnamed x7 -> x0, local copies, waits for them, and re-layouts: 5.33 us -> none
    pallas_call x0 -> x1, Pallas kernels: none -> 4.23 us  [finish(): pl.pallas_call(finish_kernel, out_shape=tuple((jax.ShapeDtypeStruct(a.sha...]
where the time goes in v2:
time: 90.8 us; the launch traced here: 90.7 us
  Pallas kernels  90.1 us (99%)
    pallas_call x1, Pallas kernels, shards(): pl.pallas_call(kernel, out_shape=(jax.ShapeDtypeStruct((tokens, width), F...  85.8 us
    pallas_call x1, Pallas kernels, finish(): pl.pallas_call(finish_kernel, out_shape=tuple((jax.ShapeDtypeStruct(a.sha...  4.23 us

profile of v2, /device:TPU:1, one launch (start us, length us, event | category | flops | bytes accessed | tf_op | source)
XLA Modules:
  0.0 90.7 jit_solution(17662698710589059461)
XLA Ops:
  0.6 85.8 %lora_step.1 = (f32[768,512]{1,0:T(8,128)}, bf16[2,384,512]{2,1,0:T(8,128)(2,1)}, bf16[64,16,512]{2,1,0:T(8,128)(2,1)}, bf16[64,16,512]{2,1,0:T(8,128)(2,1)}) custom-call(bf16[768,512]{1,0:T(8,128)(2,1)} %x_hbm.1, bf16[768,512]{1,0:T(8,128)(2,1)} %dy_hbm.1, bf16[8192,512]{1,0:T(8,128)(2,1)} %w_hbm.1, bf16[4,16,512]{2,1,0:T(8,128)(2,1)} %down_hbm.1, ...), custom_call_target="tpu_custom_call" | custom-call | tf_op jit(solution)/shard_map/lora_step/pallas_call | solution.py:637
  86.5 4.2 %finish.1 = (f32[768,512]{1,0:T(8,128)}, bf16[64,16,512]{2,1,0:T(8,128)(2,1)}, bf16[64,16,512]{2,1,0:T(8,128)(2,1)}) custom-call(f32[768,512]{1,0:T(8,128)} %get-tuple-element.7.own_in, bf16[768,512]{1,0:T(8,128)(2,1)} %bitcast.1, bf16[64,16,512]{2,1,0:T(8,128)(2,1)} %get-tuple-element.9.down_in, bf16[64,16,512]{2,1,0:T(8,128)(2,1)} %get-tuple-element.10.up_in), custom_call_target="tpu_custom_call" | custom-call | tf_op jit(solution)/shard_map/finish/pallas_call | solution.py:610

commit v3 on v2

--- a/solution.py
+++ b/solution.py
@@ -122,8 +122,8 @@
     w_hbm,
     down_hbm,
     up_hbm,
-    adapter,
-    slot_of,
+    adapter_hbm,
+    slot_of_hbm,
     own_out,
     last_out,
     down_out,
@@ -152,6 +152,8 @@
     out1,
     links_v,
     links_s,
+    adapter,
+    slot_of,
     local_sem,
     pair_send,
     pair_recv,
@@ -213,6 +215,12 @@
         pltpu.make_async_copy(x_hbm, xv, local_sem.at[3]),
     ]
     w_loads = {rel: pltpu.make_async_copy(w_rows(rel, core), wv.at[0, rel], local_sem.at[4 + rel]) for rel in W_ORDER}
+    ids_loads = [
+        pltpu.make_async_copy(adapter_hbm, adapter, local_sem.at[16]),
+        pltpu.make_async_copy(slot_of_hbm, slot_of, local_sem.at[17]),
+    ]
+    for copy in ids_loads:
+        copy.start()
     w_loads[4].start()
     loads[2].start()
     loads[0].start()
@@ -221,6 +229,8 @@
     for rel in W_ORDER[1:]:
         w_loads[rel].start()
 
+    for copy in ids_loads:
+        copy.wait()
     row = lax.broadcasted_iota(I32, (8, 128), 0)
     tile = jnp.full((8, 128), -1, I32)
     for g in range(groups):
@@ -265,81 +275,83 @@
         Gather(tab0, t0_send, t0_recv, along_x, along_y, 2),
         Gather(tab1, t1_send, t1_recv, along_y, along_x, 2),
     )
+    send_w(3)
+    send_w(5)
+
+    def frozen(rel, begin, size):
+        rows = pl.ds(begin, size)
+        dims = (((1,), (1,)), ((), ()))
+        first = lax.dot_general(dyv[0, rows], wv[0, rel], dims, preferred_element_type=F32)
+        second = lax.dot_general(dyv[1, rows], wv[1, rel], dims, preferred_element_type=F32)
+        return first + second
+
+    pieces = half // GROUP
+
+    def z_copy(way, m):
+        k, rows = m // pieces, pl.ds(m % pieces * GROUP, GROUP)
+        return pltpu.make_async_remote_copy(
+            src_ref=z_out.at[way, k, rows],
+            dst_ref=z_in.at[way, k, rows] if k < HOPS - 1 else last_out.at[way, rows],
+            send_sem=z_send.at[way, m],
+            recv_sem=z_recv.at[way, m],
+            device_id=along_z(1 - 2 * way),
+            device_id_type=MESH,
+        )
+
+    z_copies = {(way, m): z_copy(way, m) for way in range(2) for m in range(HOPS * pieces)}
+    strip = 64
+    have = set()
+
+    def z_step(m):
+        k, j = m // pieces, m % pieces
+        for way in range(2):
+            rel, begin = TARGET[way][k], HALF[way][k] * half + j * GROUP
+            if rel not in have:
+                have.add(rel)
+                w_loads[rel].wait()
+                w_pair[rel].wait_recv()
+            if k == 0:
+                dy_pair[begin].wait_recv()
+            part[way] = frozen(rel, begin, GROUP)
+            if k >= 2:
+                z_copies[way, m - 2 * pieces].wait_recv()
+
+            def move(n, carry):
+                rows = pl.ds(pl.multiple_of(j * GROUP + n * strip, strip), strip)
+                v = part[way, pl.ds(pl.multiple_of(n * strip, strip), strip)]
+                if k >= 2:
+                    v = v + decode(z_in[way, k - 2, rows])
+                z_out[way, k, rows] = encode(v)
+                return carry
+
+            lax.fori_loop(0, GROUP // strip, move, 0)
+            z_copies[way, m].start()
+
+    def z_steps(first, last):
+        for m in range(first, last + 1):
+            z_step(m)
+
+    def z_end(way, k):
+        begin = HALF[way][k] * half
+        for j in range(pieces):
+            z_copies[way, k * pieces + j].wait_recv()
+
+        def move(n, carry):
+            rows = pl.ds(pl.multiple_of(begin + n * strip, strip), strip)
+            own[rows] = own[rows] + decode(z_in[way, k, pl.ds(pl.multiple_of(n * strip, strip), strip)])
+            return carry
+
+        lax.fori_loop(0, half // strip, move, 0)
+
+    loads[2].wait()
+    z_step(0)
     loads[0].wait()
     tables[0].start()
     loads[1].wait()
     tables[1].start()
     for table in tables:
         table.across(0)
-    send_w(3)
-    send_w(5)
-
-    def frozen(rel, begin, size):
-        rows = pl.ds(begin, size)
-        dims = (((1,), (1,)), ((), ()))
-        first = lax.dot_general(dyv[0, rows], wv[0, rel], dims, preferred_element_type=F32)
-        second = lax.dot_general(dyv[1, rows], wv[1, rel], dims, preferred_element_type=F32)
-        return first + second
-
-    def z_copy(way, k, rows=pl.ds(0, half)):
-        return pltpu.make_async_remote_copy(
-            src_ref=z_out.at[way, k, rows],
-            dst_ref=z_in.at[way, k, rows] if k < HOPS - 1 else last_out.at[way, rows],
-            send_sem=z_send.at[way, k],
-            recv_sem=z_recv.at[way, k],
-            device_id=along_z(1 - 2 * way),
-            device_id_type=MESH,
-        )
-
-    z_copies = {(way, k): z_copy(way, k) for way in range(2) for k in range(HOPS)}
-    strip = 64
-    have = set()
-
-    def z_step(k):
-        for way in range(2):
-            rel = TARGET[way][k]
-            if rel not in have:
-                have.add(rel)
-                w_loads[rel].wait()
-                w_pair[rel].wait_recv()
-            part[way] = frozen(rel, HALF[way][k] * half, half)
-            if k >= 2:
-                z_copies[way, k - 2].wait_recv()
-
-            def move(n, carry):
-                rows = pl.ds(pl.multiple_of(n * strip, strip), strip)
-                v = part[way, rows]
-                if k >= 2:
-                    v = v + decode(z_in[way, k - 2, rows])
-                z_out[way, k, rows] = encode(v)
-                z_copy(way, k, rows).start()
-                return carry
-
-            lax.fori_loop(0, half // strip, move, 0)
-
-    def z_end(way, k):
-        begin = HALF[way][k] * half
-        z_copies[way, k].wait_recv()
-
-        def move(n, carry):
-            rows = pl.ds(pl.multiple_of(begin + n * strip, strip), strip)
-            own[rows] = own[rows] + decode(z_in[way, k, pl.ds(pl.multiple_of(n * strip, strip), strip)])
-            return carry
-
-        lax.fori_loop(0, half // strip, move, 0)
-
-    loads[2].wait()
-    w_loads[4].wait()
-    w_pair[4].wait_recv()
-    have.add(4)
-    for c in range(half // GROUP):
-        for way in range(2):
-            begin = HALF[way][0] * half + c * GROUP
-            dy_pair[begin].wait_recv()
-            rows = pl.ds(c * GROUP, GROUP)
-            z_out[way, 0, rows] = encode(frozen(4, begin, GROUP))
-            for n in range(GROUP // strip):
-                z_copy(way, 0, pl.ds(c * GROUP + n * strip, strip)).start()
+    z_steps(1, 2)
     for table in tables:
         table.pass_first()
         table.across(3)
@@ -357,23 +369,20 @@
 
     for k in range(1, OWNERS):
         id_copy(k, dp).start()
-    z_step(1)
+    z_steps(3, 5)
     for rel in (2, 6, 0):
         send_w(rel)
     for table in tables:
         table.end_first()
         table.across(2)
-    for i in (0, 3):
-        for table in tables:
-            table.pass_second(i)
-    z_step(2)
-    for i in (1, 2):
+    for i in (0, 3, 1, 2):
         for table in tables:
             table.pass_second(i)
     w_loads[0].wait()
     w_pair[0].wait_recv()
     for way in range(2):
         own[pl.ds(way * half, half)] = frozen(0, way * half, half)
+    z_steps(6, 7)
     for table in tables:
         table.end()
     for rel in (1, 7):
@@ -410,7 +419,7 @@
         )
         copy.start()
         r_copies.append(copy)
-    z_step(3)
+    z_steps(8, 9)
     total = rank_chip[lax.rem(z, groups)]
     for k in range(1, DEPTH):
         r_copies[k - 1].wait_recv()
@@ -443,11 +452,11 @@
     links = pltpu.make_async_copy(links_v, links_s, local_sem.at[12])
     links.start()
 
+    z_steps(10, 13)
     for k in range(1, DEPTH):
         a_copy(k, -k).wait_recv()
     halves_out = to_mate(rank_all.at[core], rank_all.at[core], 9)
     halves_out.start()
-    z_step(4)
     to_mate(rank_all.at[core], rank_all.at[1 - core], 9).wait_recv()
 
     def low_of(g):
@@ -494,22 +503,27 @@
         term = lax.dot_general(back_of(g), tab0[downs[g]], (((0,), (0,)), ((), ())), preferred_element_type=F32)
         own[rows] = own[rows] + term * SCALE_DOWN
 
-    z_step(5)
+    z_steps(14, 15)
     for grad in grads:
         grad.pass_first()
         grad.across(3)
         grad.across(1)
+    z_step(16)
     for grad in grads:
         grad.pass_second(0)
     for grad in grads:
         grad.end_first()
         grad.across(2)
-    for i in (3, 1):
-        for grad in grads:
-            grad.pass_second(i)
-    z_step(6)
+    z_step(17)
+    for grad in grads:
+        grad.pass_second(3)
+    z_step(18)
+    for grad in grads:
+        grad.pass_second(1)
+    z_step(19)
     for grad in grads:
         grad.pass_second(2)
+    z_step(20)
     for grad in grads:
         grad.end()
     for k in range(1, OWNERS):
@@ -552,7 +566,8 @@
     stores.append(pltpu.make_async_copy(own, own_out, local_sem.at[15]))
     stores[-1].start()
     for way in range(2):
-        z_copies[way, HOPS - 1].wait_recv()
+        for j in range(pieces):
+            z_copies[way, (HOPS - 1) * pieces + j].wait_recv()
     for copy in [*dy_pair.values(), rank_mate, halves_out, *w_pair.values(), *z_copies.values(), *r_copies, *a_copies]:
         copy.wait_send()
     for k in range(1, OWNERS):
@@ -565,62 +580,35 @@
 
 
 PIECES = 6
-COPIES = 4
-
-
-def finish_kernel(own_in, last_in, down_in, up_in, token_out, down_out, up_out, own, last, down, up, load_sem, store_sem):
-    def pieces(array, count):
-        size = array.shape[0] // count
-        return [pl.ds(c * size, size) for c in range(count)]
-
-    def load(j, source, target, count):
-        copies = [
-            pltpu.make_async_copy(source.at[rows], target.at[rows], load_sem.at[j, c])
-            for c, rows in enumerate(pieces(target, count))
-        ]
-        for copy in copies:
-            copy.start()
-        return copies
-
-    stores = []
-
-    def store(j, c, source, target, rows):
-        copy = pltpu.make_async_copy(source.at[rows], target.at[rows], store_sem.at[j, c])
+
+
+def finish_kernel(own, last, down, up, token_out, down_out, up_out, total, sem):
+    stores = [
+        pltpu.make_async_copy(down, down_out, sem.at[PIECES]),
+        pltpu.make_async_copy(up, up_out, sem.at[PIECES + 1]),
+    ]
+    for copy in stores:
+        copy.start()
+    size = total.shape[0] // PIECES
+    for c in range(PIECES):
+        rows = pl.ds(c * size, size)
+        total[rows] = own[rows] + decode(last[rows])
+        copy = pltpu.make_async_copy(total.at[rows], token_out.at[rows], sem.at[c])
         copy.start()
         stores.append(copy)
-
-    tables = [(load(2, down_in, down, COPIES), down, down_out), (load(3, up_in, up, COPIES), up, up_out)]
-    own_loads, last_loads = load(0, own_in, own, PIECES), load(1, last_in, last, PIECES)
-    for j, (loads, held, target) in enumerate(tables):
-        for c, rows in enumerate(pieces(held, COPIES)):
-            loads[c].wait()
-            store(1 + j, c, held, target, rows)
-    for c, rows in enumerate(pieces(own, PIECES)):
-        own_loads[c].wait()
-        last_loads[c].wait()
-        own[rows] = own[rows] + decode(last[rows])
-        store(0, c, own, token_out, rows)
     for copy in stores:
         copy.wait()
 
 
 def finish(own, last, down, up):
     any_space = pl.BlockSpec(memory_space=pl.ANY)
-    dma = pltpu.SemaphoreType.DMA
     return pl.pallas_call(
         finish_kernel,
         out_shape=tuple(jax.ShapeDtypeStruct(a.shape, a.dtype) for a in (own, down, up)),
-        in_specs=[any_space] * 4,
+        in_specs=[pl.BlockSpec(memory_space=pltpu.VMEM)] * 4,
         out_specs=(any_space,) * 3,
-        scratch_shapes=[
-            pltpu.VMEM(own.shape, F32),
-            pltpu.VMEM(last.shape, BF16),
-            pltpu.VMEM(down.shape, BF16),
-            pltpu.VMEM(up.shape, BF16),
-            dma((4, PIECES)),
-            dma((3, PIECES)),
-        ],
-        compiler_params=pltpu.CompilerParams(vmem_limit_bytes=56 * 1024 * 1024),
+        scratch_shapes=[pltpu.VMEM(own.shape, F32), pltpu.SemaphoreType.DMA((PIECES + 2,))],
+        compiler_params=pltpu.CompilerParams(vmem_limit_bytes=16 * 1024 * 1024),
         name="finish",
     )(own, last, down, up)
 
@@ -631,18 +619,17 @@
     groups = adapter.shape[0]
     slots = owned * OWNERS
     any_space = pl.BlockSpec(memory_space=pl.ANY)
-    smem = pl.BlockSpec(memory_space=pltpu.SMEM)
     dma = pltpu.SemaphoreType.DMA
     vmem = pltpu.VMEM
     own, last, stepped_down, stepped_up = pl.pallas_call(
         kernel,
         out_shape=(
-            jax.ShapeDtypeStruct((tokens, width), F32),
-            jax.ShapeDtypeStruct((2, tokens // 2, width), BF16),
-            jax.ShapeDtypeStruct((slots, rank, width), BF16),
-            jax.ShapeDtypeStruct((slots, rank, width), BF16),
+            vmem((tokens, width), F32),
+            vmem((2, tokens // 2, width), BF16),
+            vmem((slots, rank, width), BF16),
+            vmem((slots, rank, width), BF16),
         ),
-        in_specs=[any_space] * 5 + [smem] * 2,
+        in_specs=[pl.BlockSpec(memory_space=pltpu.HBM)] * 7,
         out_specs=(any_space,) * 4,
         scratch_shapes=[
             vmem((tokens, width), BF16),
@@ -658,7 +645,7 @@
             vmem((OWNERS, 8, 128), I32),
             vmem((2, HOPS, tokens // 2, width), BF16),
             vmem((2, HOPS, tokens // 2, width), BF16),
-            vmem((2, tokens // 2, width), F32),
+            vmem((2, GROUP, width), F32),
             vmem((tokens, width), F32),
             vmem((2, groups, RANK, GROUP), F32),
             vmem((groups, RANK, GROUP), F32),
@@ -669,16 +656,18 @@
             vmem((slots, rank, width), BF16),
             vmem((8, 128), I32),
             pltpu.SMEM((8, 128), I32),
-            dma((16,)),
+            pltpu.SMEM(adapter.shape, I32),
+            pltpu.SMEM(slot_of.shape, I32),
+            dma((18,)),
             dma((10 + groups,)),
             dma((10 + groups,)),
         ]
         + [dma((20,))] * 8
-        + [dma((2, HOPS))] * 2
+        + [dma((2, HOPS * (tokens // 2 // GROUP)))] * 2
         + [dma((DEPTH,))] * 4
         + [dma((OWNERS,))] * 4,
         compiler_params=pltpu.CompilerParams(
-            collective_id=0, has_side_effects=True, vmem_limit_bytes=56 * 1024 * 1024
+            collective_id=0, has_side_effects=True, vmem_limit_bytes=51 * 1024 * 1024
         ),
         name="lora_step",
     )(x, dy, w, down, up, adapter, slot_of)

time: 90.8 us -> 84.7 us (0.933)
  Pallas kernels: 90.1 us -> 83.8 us
    pallas_call x1, Pallas kernels: 85.8 us -> 81.9 us  [shards(): pl.pallas_call(kernel, out_shape=(vmem((tokens, width), F32), vmem((2, to...]
    pallas_call x1, Pallas kernels: 4.23 us -> 1.9 us  [finish(): pl.pallas_call(finish_kernel, out_shape=tuple((jax.ShapeDtypeStruct(a.sha...]
where the time goes in v3:
time: 84.7 us; the launch traced here: 84.6 us
  Pallas kernels  83.8 us (99%)
    pallas_call x1, Pallas kernels, shards(): pl.pallas_call(kernel, out_shape=(vmem((tokens, width), F32), vmem((2, to...  81.9 us
    pallas_call x1, Pallas kernels, finish(): pl.pallas_call(finish_kernel, out_shape=tuple((jax.ShapeDtypeStruct(a.sha...  1.9 us

profile of v3, /device:TPU:1, one launch (start us, length us, event | category | flops | bytes accessed | tf_op | source)
XLA Modules:
  0.0 84.6 jit_solution(12374896776171995330)
XLA Ops:
  0.6 81.9 %lora_step.1 = (f32[768,512]{1,0:T(8,128)S(1)}, bf16[2,384,512]{2,1,0:T(8,128)(2,1)S(1)}, bf16[64,16,512]{2,1,0:T(8,128)(2,1)S(1)}, bf16[64,16,512]{2,1,0:T(8,128)(2,1)S(1)}) custom-call(bf16[768,512]{1,0:T(8,128)(2,1)} %x_hbm.1, bf16[768,512]{1,0:T(8,128)(2,1)} %dy_hbm.1, bf16[8192,512]{1,0:T(8,128)(2,1)} %w_hbm.1, bf16[4,16,512]{2,1,0:T(8,128)(2,1)} %down_hbm.1, ...), custom_call_target="tpu_custom_call" | custom-call | tf_op jit(solution)/shard_map/lora_step/pallas_call | solution.py:624
  82.6 1.9 %finish.1 = (f32[768,512]{1,0:T(8,128)}, bf16[64,16,512]{2,1,0:T(8,128)(2,1)}, bf16[64,16,512]{2,1,0:T(8,128)(2,1)}) custom-call(f32[768,512]{1,0:T(8,128)S(1)} %get-tuple-element.7.own, bf16[768,512]{1,0:T(8,128)(2,1)S(1)} %bitcast.1, bf16[64,16,512]{2,1,0:T(8,128)(2,1)S(1)} %get-tuple-element.9.down, bf16[64,16,512]{2,1,0:T(8,128)(2,1)S(1)} %get-tuple-element.10.up), custom_call_target="tpu_custom_call" | custom-call | tf_op jit(solution)/shard_map/finish/pallas_call | solution.py:605

commit v4 on v3

--- a/solution.py
+++ b/solution.py
@@ -378,11 +378,7 @@
     for i in (0, 3, 1, 2):
         for table in tables:
             table.pass_second(i)
-    w_loads[0].wait()
-    w_pair[0].wait_recv()
-    for way in range(2):
-        own[pl.ds(way * half, half)] = frozen(0, way * half, half)
-    z_steps(6, 7)
+    z_step(6)
     for table in tables:
         table.end()
     for rel in (1, 7):
@@ -404,6 +400,7 @@
         rank_own[1, g] = back
     rank_mate = to_mate(rank_own.at[1 - core], rank_pair, 8)
     rank_mate.start()
+    z_step(7)
     rank_mate.wait_recv()
     rank_chip[...] = rank_own[core] + rank_pair[...]
 
@@ -419,6 +416,10 @@
         )
         copy.start()
         r_copies.append(copy)
+    w_loads[0].wait()
+    w_pair[0].wait_recv()
+    for way in range(2):
+        own[pl.ds(way * half, half)] = frozen(0, way * half, half)
     z_steps(8, 9)
     total = rank_chip[lax.rem(z, groups)]
     for k in range(1, DEPTH):
@@ -457,6 +458,7 @@
         a_copy(k, -k).wait_recv()
     halves_out = to_mate(rank_all.at[core], rank_all.at[core], 9)
     halves_out.start()
+    z_step(14)
     to_mate(rank_all.at[core], rank_all.at[1 - core], 9).wait_recv()
 
     def low_of(g):
@@ -503,7 +505,7 @@
         term = lax.dot_general(back_of(g), tab0[downs[g]], (((0,), (0,)), ((), ())), preferred_element_type=F32)
         own[rows] = own[rows] + term * SCALE_DOWN
 
-    z_steps(14, 15)
+    z_step(15)
     for grad in grads:
         grad.pass_first()
         grad.across(3)

time: 84.7 us -> 83.4 us (0.985)
  Pallas kernels: 83.8 us -> 82.6 us
    pallas_call x1, Pallas kernels: 81.9 us -> 80.7 us  [shards(): pl.pallas_call(kernel, out_shape=(vmem((tokens, width), F32), vmem((2, to...]
where the time goes in v4:
time: 83.4 us
  Pallas kernels  82.6 us (99%)
    pallas_call x1, Pallas kernels, shards(): pl.pallas_call(kernel, out_shape=(vmem((tokens, width), F32), vmem((2, to...  80.7 us
    pallas_call x1, Pallas kernels, finish(): pl.pallas_call(finish_kernel, out_shape=tuple((jax.ShapeDtypeStruct(a.sha...  1.9 us

profile of v4, /device:TPU:1, one launch (start us, length us, event | category | flops | bytes accessed | tf_op | source)
XLA Modules:
  0.0 83.4 jit_solution(10815440396340080429)
XLA Ops:
  0.6 80.7 %lora_step.1 = (f32[768,512]{1,0:T(8,128)S(1)}, bf16[2,384,512]{2,1,0:T(8,128)(2,1)S(1)}, bf16[64,16,512]{2,1,0:T(8,128)(2,1)S(1)}, bf16[64,16,512]{2,1,0:T(8,128)(2,1)S(1)}) custom-call(bf16[768,512]{1,0:T(8,128)(2,1)} %x_hbm.1, bf16[768,512]{1,0:T(8,128)(2,1)} %dy_hbm.1, bf16[8192,512]{1,0:T(8,128)(2,1)} %w_hbm.1, bf16[4,16,512]{2,1,0:T(8,128)(2,1)} %down_hbm.1, ...), custom_call_target="tpu_custom_call" | custom-call | tf_op jit(solution)/shard_map/lora_step/pallas_call | solution.py:626
  81.3 1.9 %finish.1 = (f32[768,512]{1,0:T(8,128)}, bf16[64,16,512]{2,1,0:T(8,128)(2,1)}, bf16[64,16,512]{2,1,0:T(8,128)(2,1)}) custom-call(f32[768,512]{1,0:T(8,128)S(1)} %get-tuple-element.7.own, bf16[768,512]{1,0:T(8,128)(2,1)S(1)} %bitcast.1, bf16[64,16,512]{2,1,0:T(8,128)(2,1)S(1)} %get-tuple-element.9.down, bf16[64,16,512]{2,1,0:T(8,128)(2,1)S(1)} %get-tuple-element.10.up), custom_call_target="tpu_custom_call" | custom-call | tf_op jit(solution)/shard_map/finish/pallas_call | solution.py:607

commit v5 on v4

--- a/solution.py
+++ b/solution.py
@@ -404,9 +404,10 @@
     rank_mate.wait_recv()
     rank_chip[...] = rank_own[core] + rank_pair[...]
 
-    r_copies = []
-    for k in range(1, DEPTH):
-        copy = pltpu.make_async_remote_copy(
+    far_first = (4, 3, 5, 2, 6, 1, 7)
+
+    def r_copy(k):
+        return pltpu.make_async_remote_copy(
             src_ref=rank_chip.at[lax.rem(chip_z(k), groups)],
             dst_ref=rank_in.at[k],
             send_sem=r_send.at[k],
@@ -414,18 +415,25 @@
             device_id=along_z(k),
             device_id_type=MESH,
         )
-        copy.start()
-        r_copies.append(copy)
+
+    for k in far_first:
+
+        @pl.when(chip_z(k) < groups)
+        def _():
+            r_copy(k).start()
+
     w_loads[0].wait()
     w_pair[0].wait_recv()
     for way in range(2):
         own[pl.ds(way * half, half)] = frozen(0, way * half, half)
     z_steps(8, 9)
-    total = rank_chip[lax.rem(z, groups)]
-    for k in range(1, DEPTH):
-        r_copies[k - 1].wait_recv()
-        total = total + rank_in[k]
-    rank_all[core, z] = (total * jnp.where(core == 0, SCALE_DOWN, SCALE_UP).astype(F32)).astype(BF16)
+    @pl.when(z < groups)
+    def _():
+        total = rank_chip[z]
+        for k in range(1, DEPTH):
+            r_copy(k).wait_recv()
+            total = total + rank_in[k]
+        rank_all[core, z] = (total * jnp.where(core == 0, SCALE_DOWN, SCALE_UP).astype(F32)).astype(BF16)
 
     def a_copy(k, d):
         return pltpu.make_async_remote_copy(
@@ -437,9 +445,11 @@
             device_id_type=MESH,
         )
 
-    a_copies = [a_copy(k, 0) for k in range(1, DEPTH)]
-    for copy in a_copies:
-        copy.start()
+    @pl.when(z < groups)
+    def _():
+        for k in far_first:
+            a_copy(k, 0).start()
+
     for k in range(1, OWNERS):
         id_copy(k, lax.rem(dp - k + OWNERS, OWNERS)).wait_recv()
     by_row = ids[...].reshape(OWNERS * 8, 128)
@@ -455,11 +465,16 @@
 
     z_steps(10, 13)
     for k in range(1, DEPTH):
-        a_copy(k, -k).wait_recv()
-    halves_out = to_mate(rank_all.at[core], rank_all.at[core], 9)
+
+        @pl.when(chip_z(-k) < groups)
+        def _():
+            a_copy(k, -k).wait_recv()
+
+    sums = pl.ds(0, groups)
+    halves_out = to_mate(rank_all.at[core, sums], rank_all.at[core, sums], 9)
     halves_out.start()
     z_step(14)
-    to_mate(rank_all.at[core], rank_all.at[1 - core], 9).wait_recv()
+    to_mate(rank_all.at[core, sums], rank_all.at[1 - core, sums], 9).wait_recv()
 
     def low_of(g):
         return rank_all[0, g]
@@ -570,8 +585,18 @@
     for way in range(2):
         for j in range(pieces):
             z_copies[way, (HOPS - 1) * pieces + j].wait_recv()
-    for copy in [*dy_pair.values(), rank_mate, halves_out, *w_pair.values(), *z_copies.values(), *r_copies, *a_copies]:
+    for copy in [*dy_pair.values(), rank_mate, halves_out, *w_pair.values(), *z_copies.values()]:
         copy.wait_send()
+    for k in range(1, DEPTH):
+
+        @pl.when(chip_z(k) < groups)
+        def _():
+            r_copy(k).wait_send()
+
+        @pl.when(z < groups)
+        def _():
+            a_copy(k, 0).wait_send()
+
     for k in range(1, OWNERS):
         id_copy(k, dp).wait_send()
         most_copy(k, dp).wait_send()

time: 83.4 us -> 82.7 us (level)
  Pallas kernels: 82.6 us -> 81.7 us
where the time goes in v5:
time: 82.7 us; the launch traced here: 82.5 us
  Pallas kernels  81.7 us (99%)
    pallas_call x1, Pallas kernels, shards(): pl.pallas_call(kernel, out_shape=(vmem((tokens, width), F32), vmem((2, to...  79.8 us
    pallas_call x1, Pallas kernels, finish(): pl.pallas_call(finish_kernel, out_shape=tuple((jax.ShapeDtypeStruct(a.sha...  1.9 us

profile of v5, /device:TPU:1, one launch (start us, length us, event | category | flops | bytes accessed | tf_op | source)
XLA Modules:
  0.0 82.5 jit_solution(6715041007265025120)
XLA Ops:
  0.6 79.8 %lora_step.1 = (f32[768,512]{1,0:T(8,128)S(1)}, bf16[2,384,512]{2,1,0:T(8,128)(2,1)S(1)}, bf16[64,16,512]{2,1,0:T(8,128)(2,1)S(1)}, bf16[64,16,512]{2,1,0:T(8,128)(2,1)S(1)}) custom-call(bf16[768,512]{1,0:T(8,128)(2,1)} %x_hbm.1, bf16[768,512]{1,0:T(8,128)(2,1)} %dy_hbm.1, bf16[8192,512]{1,0:T(8,128)(2,1)} %w_hbm.1, bf16[4,16,512]{2,1,0:T(8,128)(2,1)} %down_hbm.1, ...), custom_call_target="tpu_custom_call" | custom-call | tf_op jit(solution)/shard_map/lora_step/pallas_call | solution.py:651
  80.5 1.9 %finish.1 = (f32[768,512]{1,0:T(8,128)}, bf16[64,16,512]{2,1,0:T(8,128)(2,1)}, bf16[64,16,512]{2,1,0:T(8,128)(2,1)}) custom-call(f32[768,512]{1,0:T(8,128)S(1)} %get-tuple-element.7.own, bf16[768,512]{1,0:T(8,128)(2,1)S(1)} %bitcast.1, bf16[64,16,512]{2,1,0:T(8,128)(2,1)S(1)} %get-tuple-element.9.down, bf16[64,16,512]{2,1,0:T(8,128)(2,1)S(1)} %get-tuple-element.10.up), custom_call_target="tpu_custom_call" | custom-call | tf_op jit(solution)/shard_map/finish/pallas_call | solution.py:632
